TPU v7x, 128 devices: a whole 4x4x4 slice. The times are simulated.
128 devices in a mesh: section: 2 (over core), dp: 8 (over z, y_hi), tensor: 8 (over y_lo, x).
Axes of the slice: x: 4, y: 4 (y_hi: 2, y_lo: 2; y = y_hi * 2 + y_lo), z: 4, core: 2. Of those that a mesh axis runs over, the one named last changes fastest.
Arguments:
- inputs: bfloat16 [2, 576, 8, 1024], P(None, 'tensor', 'dp'), may hold values from -6 to 6
- cotangent: bfloat16 [2, 576, 8, 1024], P(None, 'tensor', 'dp'), may hold values from -6 to 6
- qkv_weight: bfloat16 [2, 1024, 3, 1024], P('section', 'dp', None, 'tensor'), may hold values from -0.1875 to 0.1875
- proj_weight: bfloat16 [2, 1024, 1024], P('section', 'tensor', 'dp'), may hold values from -0.75 to 0.75
- fc1_weight: bfloat16 [2, 1024, 4, 1024], P('section', 'dp', None, 'tensor'), may hold values from -0.1875 to 0.1875
- fc2_weight: bfloat16 [2, 4, 1024, 1024], P('section', None, 'tensor', 'dp'), may hold values from -0.09375 to 0.09375
- vectors: bfloat16 [2, 12, 1024], P('section', None, ('dp', 'tensor')), may hold values from -1.5 to 1.5
Outputs:
- activations: bfloat16 [2, 2, 576, 8, 1024], P('section', None, 'tensor', 'dp')
- grad_input: float32 [2, 2, 576, 8, 1024], P('section', None, 'tensor', 'dp')
- grad_qkv: float32 [2, 1024, 3, 1024], P('section', 'dp', None, 'tensor')
- grad_proj: float32 [2, 1024, 1024], P('section', 'tensor', 'dp')
- grad_fc1: float32 [2, 1024, 4, 1024], P('section', 'dp', None, 'tensor')
- grad_fc2: float32 [2, 4, 1024, 1024], P('section', None, 'tensor', 'dp')
- grad_vectors: float32 [2, 12, 1024], P('section', None, ('dp', 'tensor'))
All inputs are finite; a program needn't handle non-finite values.
Results may differ from a plain program's by a relative error of at most 0.019.
Values may be sent and summed in bfloat16 or wider, within the bound.
No kernel may reach another device: no remote copies, remote signals or barrier semaphores. Data moves between devices by JAX's collectives and lax.ppermute only.
A program may use at most 128 MiB of HBM per device.

v0:
```python
import jax
import jax.numpy as jnp
from jax import lax
from jax.sharding import PartitionSpec as P

HEADS = 16


eps = 1e-06
wide = jnp.float32
narrow = jnp.bfloat16


def shifted(value, axis, steps):
    count = lax.axis_size(axis)
    initial, last = (max(0, -steps), min(count, count - steps))
    return lax.ppermute(value, axis, [(source, source + steps) for source in range(initial, last)])


def layer_norm(rows, gain, shift):
    center = rows - jnp.mean(rows, axis=-1, keepdims=True)
    spread = jnp.mean(center * center, axis=-1, keepdims=True)
    return center * lax.rsqrt(spread + eps) * gain + shift


def gelu_exact(values):
    return jax.nn.gelu(values, approximate=False)


def column_total(values):
    return jnp.sum(values.astype(wide), axis=(0, 1))


def attend(queries, key_rows, value_rows, scale):
    scores = jnp.einsum("qihe,kihe->ihqk", queries, key_rows, preferred_element_type=wide) * scale
    peak = jnp.max(scores, axis=-1, keepdims=True)
    raised = jnp.exp(scores - peak)
    totals = jnp.sum(raised, axis=-1, keepdims=True)
    probs = (raised / totals).astype(narrow)
    mixed = jnp.einsum("ihqk,kihe->qihe", probs, value_rows, preferred_element_type=wide)
    return (mixed, peak + jnp.log(totals))


def attend_back(queries, key_rows, value_rows, log_total, mixed_grad, scale):
    scores = jnp.einsum("qihe,kihe->ihqk", queries, key_rows, preferred_element_type=wide) * scale
    probs = jnp.exp(scores - log_total)
    value_grad = jnp.einsum(
        "ihqk,qihe->kihe", probs.astype(narrow), mixed_grad, preferred_element_type=wide
    )
    prob_grad = jnp.einsum("qihe,kihe->ihqk", mixed_grad, value_rows, preferred_element_type=wide)
    score_grad = (probs * (prob_grad - jnp.sum(probs * prob_grad, axis=-1, keepdims=True))).astype(
        narrow
    )
    query_grad = (
        jnp.einsum("ihqk,kihe->qihe", score_grad, key_rows, preferred_element_type=wide) * scale
    )
    key_grad = (
        jnp.einsum("ihqk,qihe->kihe", score_grad, queries, preferred_element_type=wide) * scale
    )
    return (query_grad, key_grad, value_grad)


def spread_in(rows_low, matrix):
    return jnp.einsum(
        "sid,de->sie",
        lax.all_gather(rows_low, "tensor", axis=0, tiled=True),
        matrix,
        preferred_element_type=wide,
    )


def gather_out(full_low, matrix):
    return lax.psum_scatter(
        jnp.einsum("sie,ed->sid", full_low, matrix, preferred_element_type=wide).astype(
            jnp.bfloat16
        ),
        "tensor",
        scatter_dimension=0,
        tiled=True,
    ).astype(jnp.float32)


def spread_back(grad_low, matrix, kept_low):
    piece = lax.all_gather(grad_low, "tensor", axis=0, tiled=True)
    back_rows = jnp.einsum("sid,ed->sie", piece, matrix, preferred_element_type=wide)
    weight_total = jnp.einsum("sie,sid->ed", kept_low, piece, preferred_element_type=wide)
    return (back_rows, weight_total)


def weight_back(rows_low, grad_full):
    return jnp.einsum(
        "sid,sie->de",
        lax.all_gather(rows_low, "tensor", axis=0, tiled=True),
        grad_full,
        preferred_element_type=wide,
    )


def input_back(grad_full, matrix):
    return lax.psum_scatter(
        jnp.einsum("sie,de->sid", grad_full, matrix, preferred_element_type=wide).astype(
            jnp.bfloat16
        ),
        "tensor",
        scatter_dimension=0,
        tiled=True,
    ).astype(jnp.float32)


def per_device(inputs, cotangent, qkv_weight, proj_weight, fc1_weight, fc2_weight, vectors):
    micro = inputs.shape[0]
    seq_local = inputs.shape[1]
    images = inputs.shape[2]
    width = inputs.shape[3]
    parts = lax.axis_size("tensor")
    local_width = width // parts
    head_dim = width // HEADS
    heads_local = local_width // head_dim
    scale = head_dim ** (-0.5)
    seq_full = seq_local * parts
    section_index = lax.axis_index("section")
    tensor_index = lax.axis_index("tensor")

    def shaped(matrices):
        return (
            matrices[0].reshape(width, 3 * local_width),
            matrices[1],
            matrices[2].reshape(width, 4 * local_width),
            matrices[3].reshape(4 * local_width, width),
        )

    def owner_shapes(qkv_grad, proj_grad, fc1_grad, fc2_grad):
        return (
            qkv_grad.reshape(width, 3, local_width),
            proj_grad,
            fc1_grad.reshape(width, 4, local_width),
            fc2_grad.reshape(4, local_width, width),
        )

    gathered = (
        lax.all_gather(qkv_weight[0], "dp", axis=0, tiled=True),
        lax.all_gather(proj_weight[0], "dp", axis=1, tiled=True),
        lax.all_gather(fc1_weight[0], "dp", axis=0, tiled=True),
        lax.all_gather(fc2_weight[0], "dp", axis=2, tiled=True),
    )
    table = lax.all_gather(vectors[0], ("dp", "tensor"), axis=1, tiled=True).astype(wide)
    column_bias = lax.dynamic_slice_in_dim(table[6:12], tensor_index * local_width, local_width, 1)
    qkv_bias = jnp.stack([column_bias[0], jnp.zeros_like(column_bias[0]), column_bias[1]]).reshape(
        3 * local_width
    )
    fc1_bias = column_bias[2:6].reshape(4 * local_width)
    mats_forward = shaped(gathered)
    received = jnp.zeros((seq_local, images, width), narrow)
    sent_list = []
    kept_list = []
    for tick in range(micro + 1):
        arriving = jnp.where(section_index == 0, inputs[min(tick, micro - 1)], received)
        forward_arriving = arriving.astype(wide)
        forward_qkv_mat, forward_proj_mat, forward_fc1_mat, forward_fc2_mat = mats_forward
        forward_normed = layer_norm(forward_arriving, table[0], table[1]).astype(narrow)
        forward_projected = (spread_in(forward_normed, forward_qkv_mat) + qkv_bias).astype(narrow)
        forward_split = forward_projected.reshape(seq_full, images, 3, heads_local, head_dim)
        mixed, forward_log_total = attend(
            forward_split[:, :, 0], forward_split[:, :, 1], forward_split[:, :, 2], scale
        )
        forward_mixed_low = mixed.reshape(seq_full, images, local_width).astype(narrow)
        forward_middle = (
            forward_arriving + gather_out(forward_mixed_low, forward_proj_mat) + table[4]
        )
        forward_second = layer_norm(forward_middle, table[2], table[3]).astype(narrow)
        forward_hidden = spread_in(forward_second, forward_fc1_mat) + fc1_bias
        forward_activated = gelu_exact(forward_hidden).astype(narrow)
        leaving = forward_middle + gather_out(forward_activated, forward_fc2_mat) + table[5]
        leaving, kept = (
            leaving,
            (
                forward_normed,
                forward_projected,
                forward_log_total,
                forward_mixed_low,
                forward_middle,
                forward_second,
                forward_hidden,
                forward_activated,
            ),
        )
        sent = leaving.astype(narrow)
        sent_list.append(sent)
        kept_list.append((arriving, kept))
        if tick < micro:
            received = shifted(sent, "section", 1)
    sent_stack = jnp.stack(sent_list)
    kept_stack = jax.tree.map(lambda *leaves: jnp.stack(leaves), *kept_list)
    mats_backward = shaped(
        (
            lax.all_gather(qkv_weight[0], "dp", axis=0, tiled=True),
            lax.all_gather(proj_weight[0], "dp", axis=1, tiled=True),
            lax.all_gather(fc1_weight[0], "dp", axis=0, tiled=True),
            lax.all_gather(fc2_weight[0], "dp", axis=2, tiled=True),
        )
    )
    owned = tuple(
        (
            jnp.zeros(weight.shape[1:], wide)
            for weight in (qkv_weight, proj_weight, fc1_weight, fc2_weight)
        )
    )
    summed = owner_shapes(
        jnp.zeros((width, 3 * local_width), wide),
        jnp.zeros((local_width, width), wide),
        jnp.zeros((width, 4 * local_width), wide),
        jnp.zeros((4 * local_width, width), wide),
    )
    vector_total = jnp.zeros((12, width), wide)
    upstream = jnp.zeros((seq_local, images, width), narrow)
    grad_list = []
    for tick in range(micro + 1):
        grad = jnp.where(section_index == 1, cotangent[min(tick, micro - 1)], upstream).astype(wide)
        source = jnp.clip(tick - 1 + 2 * section_index, 0, micro)
        arriving, kept = jax.tree.map(
            lambda leaf: lax.dynamic_index_in_dim(leaf, source, 0, keepdims=False), kept_stack
        )
        backward_arriving = arriving.astype(wide)
        normed, projected, log_total, mixed_low, middle, second, hidden, activated = kept
        qkv_mat, proj_mat, fc1_mat, fc2_mat = mats_backward
        down_grad = grad.astype(narrow)
        act_grad, fc2_part = spread_back(down_grad, fc2_mat, activated)
        unused, gelu_pull = jax.vjp(gelu_exact, hidden)
        hidden_grad = gelu_pull(act_grad)[0].astype(narrow)
        second_grad = input_back(hidden_grad, fc1_mat)
        unused, norm_pull = jax.vjp(layer_norm, middle, table[2], table[3])
        middle_part, gain_two, shift_two = norm_pull(second_grad)
        middle_grad = grad + middle_part
        branch_grad = middle_grad.astype(narrow)
        mixed_grad, proj_part = spread_back(branch_grad, proj_mat, mixed_low)
        split = projected.reshape(seq_full, images, 3, heads_local, head_dim)
        mixed_grad = mixed_grad.astype(narrow).reshape(seq_full, images, heads_local, head_dim)
        query_grad, key_grad, value_grad = attend_back(
            split[:, :, 0], split[:, :, 1], split[:, :, 2], log_total, mixed_grad, scale
        )
        projected_grad = (
            jnp.stack([query_grad, key_grad, value_grad], axis=2)
            .reshape(seq_full, images, 3 * local_width)
            .astype(narrow)
        )
        normed_grad = input_back(projected_grad, qkv_mat)
        unused, first_pull = jax.vjp(layer_norm, backward_arriving, table[0], table[1])
        arriving_part, gain_one, shift_one = first_pull(normed_grad)
        projected_sums = column_total(projected_grad).reshape(3, local_width)
        hidden_sums = column_total(hidden_grad).reshape(4, local_width)
        local_rows = jnp.concatenate(
            [projected_sums[0:1], projected_sums[2:3], hidden_sums], axis=0
        )
        placed = lax.dynamic_update_slice_in_dim(
            jnp.zeros((6, width), wide), local_rows, tensor_index * local_width, 1
        )
        shared_rows = jnp.stack(
            [
                gain_one,
                shift_one,
                gain_two,
                shift_two,
                column_total(branch_grad),
                column_total(down_grad),
            ]
        )
        vector_grad = jnp.concatenate([shared_rows, placed], axis=0)
        backward_fc1_grad = weight_back(second, hidden_grad)
        backward_qkv_grad = weight_back(normed, projected_grad)
        result = owner_shapes(backward_qkv_grad, proj_part, backward_fc1_grad, fc2_part)
        input_grad, result, vector_grad = (middle_grad + arriving_part, result, vector_grad)
        batch_index = tick - 1 + section_index
        live = (batch_index >= 0) & (batch_index < micro)
        vector_total = vector_total + jnp.where(live, vector_grad, 0.0)
        grad_list.append(input_grad)
        if tick < micro:
            upstream = shifted(input_grad.astype(narrow), "section", -1)
        weight_grads = tuple((jnp.where(live, leaf, 0.0) for leaf in result))
        reduce_owned = owned
        pieces = (
            lax.psum_scatter(
                weight_grads[0].astype(jnp.bfloat16), "dp", scatter_dimension=0, tiled=True
            ).astype(jnp.float32),
            lax.psum_scatter(
                weight_grads[1].astype(jnp.bfloat16), "dp", scatter_dimension=1, tiled=True
            ).astype(jnp.float32),
            lax.psum_scatter(
                weight_grads[2].astype(jnp.bfloat16), "dp", scatter_dimension=0, tiled=True
            ).astype(jnp.float32),
            lax.psum_scatter(
                weight_grads[3].astype(jnp.bfloat16), "dp", scatter_dimension=2, tiled=True
            ).astype(jnp.float32),
        )
        reduce_owned = tuple((total + piece for total, piece in zip(reduce_owned, pieces)))
        owned, summed = (reduce_owned, summed)
    vector_owned = lax.psum_scatter(vector_total, ("dp", "tensor"), scatter_dimension=1, tiled=True)
    grad_stack = jnp.stack(grad_list)
    activations = jnp.stack(
        [
            lax.dynamic_index_in_dim(sent_stack, batch + section_index, 0, keepdims=False)
            for batch in range(micro)
        ]
    )
    grad_input = jnp.stack(
        [
            lax.dynamic_index_in_dim(grad_stack, batch + 1 - section_index, 0, keepdims=False)
            for batch in range(micro)
        ]
    )
    return (
        activations[None],
        grad_input[None],
        owned[0][None],
        owned[1][None],
        owned[2][None],
        owned[3][None],
        vector_owned[None],
    )


def solution(mesh):
    in_specs = (
        P(None, "tensor", "dp", None),
        P(None, "tensor", "dp", None),
        P("section", "dp", None, "tensor"),
        P("section", "tensor", "dp"),
        P("section", "dp", None, "tensor"),
        P("section", None, "tensor", "dp"),
        P("section", None, ("dp", "tensor")),
    )
    out_specs = (
        P("section", None, "tensor", "dp", None),
        P("section", None, "tensor", "dp", None),
        P("section", "dp", None, "tensor"),
        P("section", "tensor", "dp"),
        P("section", "dp", None, "tensor"),
        P("section", None, "tensor", "dp"),
        P("section", None, ("dp", "tensor")),
    )
    return jax.shard_map(
        per_device, mesh=mesh, in_specs=in_specs, out_specs=out_specs, check_vma=False
    )
```

profile of v0, /device:TPU:0, one launch (start us, length us, event | category | flops | bytes accessed | tf_op | source)
XLA Modules:
  0.0 2806.5 jit_solution(10900267797167433779)
XLA Ops:
  8.8 180.7 %all-gather = bf16[1,12,1024]{1,0,2:T(2,128)(2,1)S(1)} all-gather(bf16[1,12,16]{1,0,2:T(2,128)(2,1)S(1)} %copy.118), channel_id=2, replica_groups=mesh['section'=2,'dp'=8,'tensor'=8] {'dp','tensor'}, dimensions={2}, use_global_device_ids=true | all-gather | bytes 24960 | tf_op jit(solution)/shard_map/all_gather | solution.py:146
  332.2 38.8 %all-gather.35.cloned.1.call-done = bf16[576,1,1024]{2,0,1:T(8,128)(2,1)} async-done(((bf16[72,1,1024]{2,0,1:T(8,128)(2,1)}), bf16[576,1,1024]{2,0,1:T(8,128)(2,1)}) %all-gather.35.cloned.1.call-update) | async-done | bytes 1179664 | tf_op jit(solution)/shard_map/all_gather | solution.py:66
  376.9 40.6 %all-gather.57.cloned.1.call-done = bf16[1,4,128,1024]{3,2,1,0:T(8,128)(2,1)} async-done(((bf16[1,4,128,128]{3,2,1,0:T(8,128)(2,1)}), bf16[1,4,128,1024]{3,2,1,0:T(8,128)(2,1)}) %all-gather.57.cloned.1.call-update) | async-done | bytes 1048592 | tf_op jit(solution)/shard_map/all_gather | solution.py:144
  420.8 37.7 %reduce-scatter.42.cloned.1.call-done = bf16[72,1,1024]{2,0,1:T(8,128)(2,1)} async-done(((bf16[576,1,1024]{2,0,1:T(8,128)(2,1)}), bf16[72,1,1024]{2,0,1:T(8,128)(2,1)}) %reduce-scatter.42.cloned.1.call-update) | async-done | bytes 147472 | tf_op jit(solution)/shard_map/reduce_scatter | solution.py:73
  463.1 38.2 %all-gather.37.cloned.1.call-done = bf16[576,1,1024]{2,0,1:T(8,128)(2,1)} async-done(((bf16[72,1,1024]{2,0,1:T(8,128)(2,1)}), bf16[576,1,1024]{2,0,1:T(8,128)(2,1)}) %all-gather.37.cloned.1.call-update) | async-done | bytes 1179664 | tf_op jit(solution)/shard_map/all_gather | solution.py:66
  507.2 38.7 %reduce-scatter.44.cloned.1.call-done = bf16[72,1,1024]{2,0,1:T(8,128)(2,1)} async-done(((bf16[576,1,1024]{2,0,1:T(8,128)(2,1)}), bf16[72,1,1024]{2,0,1:T(8,128)(2,1)}) %reduce-scatter.44.cloned.1.call-update) | async-done | bytes 147472 | tf_op jit(solution)/shard_map/reduce_scatter | solution.py:73
  550.1 38.0 %all-gather.39.cloned.1.call-done = bf16[576,1,1024]{2,0,1:T(8,128)(2,1)} async-done(((bf16[72,1,1024]{2,0,1:T(8,128)(2,1)}), bf16[576,1,1024]{2,0,1:T(8,128)(2,1)}) %all-gather.39.cloned.1.call-update) | async-done | bytes 1179664 | tf_op jit(solution)/shard_map/all_gather | solution.py:66
  596.7 38.7 %reduce-scatter.46.cloned.1.call-done = bf16[72,1,1024]{2,0,1:T(8,128)(2,1)} async-done(((bf16[576,1,1024]{2,0,1:T(8,128)(2,1)}), bf16[72,1,1024]{2,0,1:T(8,128)(2,1)}) %reduce-scatter.46.cloned.1.call-update) | async-done | bytes 147472 | tf_op jit(solution)/shard_map/reduce_scatter | solution.py:73
  640.0 38.2 %all-gather.41.cloned.1.call-done = bf16[576,1,1024]{2,0,1:T(8,128)(2,1)} async-done(((bf16[72,1,1024]{2,0,1:T(8,128)(2,1)}), bf16[576,1,1024]{2,0,1:T(8,128)(2,1)}) %all-gather.41.cloned.1.call-update) | async-done | bytes 1179664 | tf_op jit(solution)/shard_map/all_gather | solution.py:66
  684.0 38.7 %reduce-scatter.48.cloned.1.call-done = bf16[72,1,1024]{2,0,1:T(8,128)(2,1)} async-done(((bf16[576,1,1024]{2,0,1:T(8,128)(2,1)}), bf16[72,1,1024]{2,0,1:T(8,128)(2,1)}) %reduce-scatter.48.cloned.1.call-update) | async-done | bytes 147472 | tf_op jit(solution)/shard_map/reduce_scatter | solution.py:73
  814.9 37.2 %reduce-scatter.52.cloned.1.call-done = bf16[72,1,1024]{2,0,1:T(8,128)(2,1)} async-done(((bf16[576,1,1024]{2,0,1:T(8,128)(2,1)}), bf16[72,1,1024]{2,0,1:T(8,128)(2,1)}) %reduce-scatter.52.cloned.1.call-update) | async-done | bytes 147472 | tf_op jit(solution)/shard_map/reduce_scatter | solution.py:100
  908.2 37.1 %reduce-scatter.54.cloned.1.call-done = bf16[72,1,1024]{2,0,1:T(8,128)(2,1)} async-done(((bf16[576,1,1024]{2,0,1:T(8,128)(2,1)}), bf16[72,1,1024]{2,0,1:T(8,128)(2,1)}) %reduce-scatter.54.cloned.1.call-update) | async-done | bytes 147472 | tf_op jit(solution)/shard_map/reduce_scatter | solution.py:100
  953.6 38.2 %all-gather.47.cloned.1.call-done = bf16[576,1,1024]{2,0,1:T(8,128)(2,1)} async-done(((bf16[72,1,1024]{2,0,1:T(8,128)(2,1)}), bf16[576,1,1024]{2,0,1:T(8,128)(2,1)}) %all-gather.47.cloned.1.call-update) | async-done | bytes 1179664 | tf_op jit(solution)/shard_map/all_gather | solution.py:84
  1000.7 38.2 %reduce-scatter.56.cloned.1.call-done = bf16[72,1,1024]{2,0,1:T(8,128)(2,1)} async-done(((bf16[576,1,1024]{2,0,1:T(8,128)(2,1)}), bf16[72,1,1024]{2,0,1:T(8,128)(2,1)}) %reduce-scatter.56.cloned.1.call-update) | async-done | bytes 147472 | tf_op jit(solution)/shard_map/reduce_scatter | solution.py:100
  1094.1 38.2 %reduce-scatter.58.cloned.1.call-done = bf16[72,1,1024]{2,0,1:T(8,128)(2,1)} async-done(((bf16[576,1,1024]{2,0,1:T(8,128)(2,1)}), bf16[72,1,1024]{2,0,1:T(8,128)(2,1)}) %reduce-scatter.58.cloned.1.call-update) | async-done | bytes 147472 | tf_op jit(solution)/shard_map/reduce_scatter | solution.py:100
  1141.6 38.1 %all-gather.51.cloned.1.call-done = bf16[576,1,1024]{2,0,1:T(8,128)(2,1)} async-done(((bf16[72,1,1024]{2,0,1:T(8,128)(2,1)}), bf16[576,1,1024]{2,0,1:T(8,128)(2,1)}) %all-gather.51.cloned.1.call-update) | async-done | bytes 1179664 | tf_op jit(solution)/shard_map/all_gather | solution.py:84
  1352.4 38.2 %all-gather.61.cloned.1.call-done = bf16[1,576,1,1024]{3,1,2,0:T(8,128)(2,1)} async-done(((bf16[1,72,1,1024]{3,1,2,0:T(8,128)(2,1)}), bf16[1,576,1,1024]{3,1,2,0:T(8,128)(2,1)}) %all-gather.61.cloned.1.call-update) | async-done | bytes 1179664 | tf_op jit(solution)/shard_map/all_gather | solution.py:93
  1474.0 71.5 %reduce-scatter.82.cloned.1.call-done = bf16[128,512]{1,0:T(8,128)(2,1)} async-done(((bf16[1024,512]{1,0:T(8,128)(2,1)}), bf16[128,512]{1,0:T(8,128)(2,1)}) %reduce-scatter.82.cloned.1.call-update) | async-done | bytes 131088
  1548.6 37.8 %reduce-scatter.50.cloned.1.call-done = bf16[72,1,1024]{2,0,1:T(8,128)(2,1)} async-done(((bf16[576,1,1024]{2,0,1:T(8,128)(2,1)}), bf16[72,1,1024]{2,0,1:T(8,128)(2,1)}) %reduce-scatter.50.cloned.1.call-update) | async-done | bytes 147472 | tf_op jit(solution)/shard_map/reduce_scatter | solution.py:73
  1588.5 70.9 %reduce-scatter.76.cloned.1.call-done = bf16[128,128]{1,0:T(8,128)(2,1)} async-done(((bf16[1024,128]{1,0:T(8,128)(2,1)}), bf16[128,128]{1,0:T(8,128)(2,1)}) %reduce-scatter.76.cloned.1.call-update) | async-done | bytes 32784
  1660.5 73.8 %reduce-scatter.84.cloned.1.call-done = bf16[128,512]{1,0:T(8,128)(2,1)} async-done(((bf16[1024,512]{1,0:T(8,128)(2,1)}), bf16[128,512]{1,0:T(8,128)(2,1)}) %reduce-scatter.84.cloned.1.call-update) | async-done | bytes 131088
  1735.5 71.8 %reduce-scatter.78.cloned.1.call-done = bf16[128,128]{1,0:T(8,128)(2,1)} async-done(((bf16[1024,128]{1,0:T(8,128)(2,1)}), bf16[128,128]{1,0:T(8,128)(2,1)}) %reduce-scatter.78.cloned.1.call-update) | async-done | bytes 32784
  1808.4 73.8 %reduce-scatter.70.cloned.1.call-done = bf16[128,4,128]{2,0,1:T(8,128)(2,1)} async-done(((bf16[1024,4,128]{2,0,1:T(8,128)(2,1)}), bf16[128,4,128]{2,0,1:T(8,128)(2,1)}) %reduce-scatter.70.cloned.1.call-update) | async-done | bytes 131088 | tf_op jit(solution)/shard_map/reduce_scatter | solution.py:287
  1882.2 75.4 %reduce-scatter.72.cloned.1.call-done = bf16[128,4,128]{2,0,1:T(8,128)(2,1)} async-done(((bf16[1024,4,128]{2,0,1:T(8,128)(2,1)}), bf16[128,4,128]{2,0,1:T(8,128)(2,1)}) %reduce-scatter.72.cloned.1.call-update) | async-done | bytes 131088 | tf_op jit(solution)/shard_map/reduce_scatter | solution.py:287
  1957.5 75.0 %reduce-scatter.74.cloned.1.call-done = bf16[128,4,128]{2,0,1:T(8,128)(2,1)} async-done(((bf16[1024,4,128]{2,0,1:T(8,128)(2,1)}), bf16[128,4,128]{2,0,1:T(8,128)(2,1)}) %reduce-scatter.74.cloned.1.call-update) | async-done | bytes 131088 | tf_op jit(solution)/shard_map/reduce_scatter | solution.py:287
  2034.5 72.8 %reduce-scatter.86.cloned.1.call-done = bf16[128,512]{1,0:T(8,128)(2,1)} async-done(((bf16[1024,512]{1,0:T(8,128)(2,1)}), bf16[128,512]{1,0:T(8,128)(2,1)}) %reduce-scatter.86.cloned.1.call-update) | async-done | bytes 131088
  2109.3 70.3 %reduce-scatter.80.cloned.1.call-done = bf16[128,128]{1,0:T(8,128)(2,1)} async-done(((bf16[1024,128]{1,0:T(8,128)(2,1)}), bf16[128,128]{1,0:T(8,128)(2,1)}) %reduce-scatter.80.cloned.1.call-update) | async-done | bytes 32784
  2181.2 72.8 %reduce-scatter.64.cloned.1.call-done = bf16[128,3,128]{2,0,1:T(8,128)(2,1)} async-done(((bf16[1024,3,128]{2,0,1:T(8,128)(2,1)}), bf16[128,3,128]{2,0,1:T(8,128)(2,1)}) %reduce-scatter.64.cloned.1.call-update) | async-done | bytes 98320 | tf_op jit(solution)/shard_map/reduce_scatter | solution.py:281
  2254.0 74.6 %reduce-scatter.66.cloned.1.call-done = bf16[128,3,128]{2,0,1:T(8,128)(2,1)} async-done(((bf16[1024,3,128]{2,0,1:T(8,128)(2,1)}), bf16[128,3,128]{2,0,1:T(8,128)(2,1)}) %reduce-scatter.66.cloned.1.call-update) | async-done | bytes 98320 | tf_op jit(solution)/shard_map/reduce_scatter | solution.py:281
  2328.6 74.2 %reduce-scatter.68.cloned.1.call-done = bf16[128,3,128]{2,0,1:T(8,128)(2,1)} async-done(((bf16[1024,3,128]{2,0,1:T(8,128)(2,1)}), bf16[128,3,128]{2,0,1:T(8,128)(2,1)}) %reduce-scatter.68.cloned.1.call-update) | async-done | bytes 98320 | tf_op jit(solution)/shard_map/reduce_scatter | solution.py:281
  2404.4 39.2 %reduce-scatter.62.cloned.1.call-done = bf16[72,1,1024]{2,0,1:T(8,128)(2,1)} async-done(((bf16[576,1,1024]{2,0,1:T(8,128)(2,1)}), bf16[72,1,1024]{2,0,1:T(8,128)(2,1)}) %reduce-scatter.62.cloned.1.call-update) | async-done | bytes 147472 | tf_op jit(solution)/shard_map/reduce_scatter | solution.py:100
  2449.3 348.0 %reduce-scatter.88.cloned.1.call-done = f32[16,12]{1,0:T(8,128)} async-done(((f32[1024,12]{1,0:T(8,128)}), f32[16,12]{1,0:T(8,128)}) %reduce-scatter.88.cloned.1.call-update) | async-done | bytes 784
  (647 shorter events, 692.6 us)
Async XLA Ops:
  8.0 272.1 %all-gather.33.cloned.1.call-start = ((), (), s32[]{:S(2)}) async-start(), calls=%async_computation.25 | async-start | bytes 1327104 | tf_op jit(solution)/shard_map/all_gather | solution.py:66
  208.5 111.7 %reduce-scatter.40.cloned.1.call-start = ((), (), s32[]{:S(2)}) async-start(), calls=%async_computation.26 | async-start | bytes 1327104 | tf_op jit(solution)/shard_map/reduce_scatter | solution.py:73
  324.1 93.4 %all-gather.57.cloned.1.call-start = ((), (), s32[]{:S(2)}) async-start(), calls=%async_computation.55 | async-start | bytes 1179648 | tf_op jit(solution)/shard_map/all_gather | solution.py:144
  324.7 133.8 %reduce-scatter.42.cloned.1.call-start = ((), (), s32[]{:S(2)}) async-start(), calls=%async_computation.28 | async-start | bytes 1327104 | tf_op jit(solution)/shard_map/reduce_scatter | solution.py:73
  549.9 85.5 %reduce-scatter.46.cloned.1.call-start = ((), (), s32[]{:S(2)}) async-start(), calls=%async_computation.32 | async-start | bytes 1327104 | tf_op jit(solution)/shard_map/reduce_scatter | solution.py:73
  728.7 123.4 %reduce-scatter.52.cloned.1.call-start = ((), (), s32[]{:S(2)}) async-start(), calls=%async_computation.37 | async-start | bytes 1327104 | tf_op jit(solution)/shard_map/reduce_scatter | solution.py:100
  856.7 88.6 %reduce-scatter.54.cloned.1.call-start = ((), (), s32[]{:S(2)}) async-start(), calls=%async_computation.39 | async-start | bytes 1327104 | tf_op jit(solution)/shard_map/reduce_scatter | solution.py:100
  906.5 85.2 %all-gather.47.cloned.1.call-start = ((), (), s32[]{:S(2)}) async-start(), calls=%async_computation.40 | async-start | bytes 1327104 | tf_op jit(solution)/shard_map/all_gather | solution.py:84
  953.5 85.3 %reduce-scatter.56.cloned.1.call-start = ((), (), s32[]{:S(2)}) async-start(), calls=%async_computation.41 | async-start | bytes 1327104 | tf_op jit(solution)/shard_map/reduce_scatter | solution.py:100
  1043.8 88.5 %reduce-scatter.58.cloned.1.call-start = ((), (), s32[]{:S(2)}) async-start(), calls=%async_computation.43 | async-start | bytes 1327104 | tf_op jit(solution)/shard_map/reduce_scatter | solution.py:100
  1093.5 86.2 %all-gather.51.cloned.1.call-start = ((), (), s32[]{:S(2)}) async-start(), calls=%async_computation.44 | async-start | bytes 1327104 | tf_op jit(solution)/shard_map/all_gather | solution.py:84
  1141.5 86.4 %reduce-scatter.60.cloned.1.call-start = ((), (), s32[]{:S(2)}) async-start(), calls=%async_computation.45 | async-start | bytes 1327104 | tf_op jit(solution)/shard_map/reduce_scatter | solution.py:100
  1190.6 118.5 %all-gather.71.cloned.1.call-start = ((), (), s32[]{:S(2)}) async-start(), calls=%async_computation.62 | async-start | bytes 1327104 | tf_op jit(solution)/shard_map/all_gather | solution.py:93
  1191.3 158.5 %all-gather.53.cloned.1.call-start = ((), (), s32[]{:S(2)}) async-start(), calls=%async_computation.46 | async-start | bytes 1327104 | tf_op jit(solution)/shard_map/all_gather | solution.py:84
  1232.8 157.8 %all-gather.61.cloned.1.call-start = ((), (), s32[]{:S(2)}) async-start(), calls=%async_computation.57 | async-start | bytes 1327104 | tf_op jit(solution)/shard_map/all_gather | solution.py:93
  1234.2 196.5 %all-gather.63.cloned.1.call-start = ((), (), s32[]{:S(2)}) async-start(), calls=%async_computation.58 | async-start | bytes 1327104 | tf_op jit(solution)/shard_map/all_gather | solution.py:93
  1235.0 235.8 %all-gather.65.cloned.1.call-start = ((), (), s32[]{:S(2)}) async-start(), calls=%async_computation.59 | async-start | bytes 1327104 | tf_op jit(solution)/shard_map/all_gather | solution.py:93
  1235.6 310.0 %reduce-scatter.82.cloned.1.call-start = ((), (), s32[]{:S(2)}) async-start(), calls=%async_computation.66 | async-start | bytes 1179648
  1240.2 346.2 %reduce-scatter.50.cloned.1.call-start = ((), (), s32[]{:S(2)}) async-start(), calls=%async_computation.36 | async-start | bytes 1327104 | tf_op jit(solution)/shard_map/reduce_scatter | solution.py:73
  1243.4 416.1 %reduce-scatter.76.cloned.1.call-start = ((), (), s32[]{:S(2)}) async-start(), calls=%async_computation.63 | async-start | bytes 294912
  1245.9 488.4 %reduce-scatter.84.cloned.1.call-start = ((), (), s32[]{:S(2)}) async-start(), calls=%async_computation.67 | async-start | bytes 1179648
  1250.2 557.1 %reduce-scatter.78.cloned.1.call-start = ((), (), s32[]{:S(2)}) async-start(), calls=%async_computation.64 | async-start | bytes 294912
  1251.9 630.3 %reduce-scatter.70.cloned.1.call-start = ((), (), s32[]{:S(2)}) async-start(), calls=%async_computation.51 | async-start | bytes 1179648 | tf_op jit(solution)/shard_map/reduce_scatter | solution.py:287
  1255.3 702.2 %reduce-scatter.72.cloned.1.call-start = ((), (), s32[]{:S(2)}) async-start(), calls=%async_computation.52 | async-start | bytes 1179648 | tf_op jit(solution)/shard_map/reduce_scatter | solution.py:287
  1272.2 760.3 %reduce-scatter.74.cloned.1.call-start = ((), (), s32[]{:S(2)}) async-start(), calls=%async_computation.53 | async-start | bytes 1179648 | tf_op jit(solution)/shard_map/reduce_scatter | solution.py:287
  1312.4 794.9 %reduce-scatter.86.cloned.1.call-start = ((), (), s32[]{:S(2)}) async-start(), calls=%async_computation.68 | async-start | bytes 1179648
  1316.7 863.0 %reduce-scatter.80.cloned.1.call-start = ((), (), s32[]{:S(2)}) async-start(), calls=%async_computation.65 | async-start | bytes 294912
  1352.4 901.6 %reduce-scatter.64.cloned.1.call-start = ((), (), s32[]{:S(2)}) async-start(), calls=%async_computation.48 | async-start | bytes 884736 | tf_op jit(solution)/shard_map/reduce_scatter | solution.py:281
  1393.8 934.8 %reduce-scatter.66.cloned.1.call-start = ((), (), s32[]{:S(2)}) async-start(), calls=%async_computation.49 | async-start | bytes 884736 | tf_op jit(solution)/shard_map/reduce_scatter | solution.py:281
  1434.0 968.7 %reduce-scatter.68.cloned.1.call-start = ((), (), s32[]{:S(2)}) async-start(), calls=%async_computation.50 | async-start | bytes 884736 | tf_op jit(solution)/shard_map/reduce_scatter | solution.py:281
  1474.0 969.7 %reduce-scatter.62.cloned.1.call-start = ((), (), s32[]{:S(2)}) async-start(), calls=%async_computation.47 | async-start | bytes 1327104 | tf_op jit(solution)/shard_map/reduce_scatter | solution.py:100
  1548.5 1248.7 %reduce-scatter.88.cloned.1.call-start = ((), (), s32[]{:S(2)}) async-start(), calls=%async_computation.69 | async-start | bytes 532480
  (167 other events, 9591.3 us)
Sparse Core Ops, SparseCore 0:
  208.6 32.5 all-gather.32
  286.4 33.7 reduce-scatter.39
  420.9 37.5 reduce-scatter.41
  507.3 38.6 reduce-scatter.43
  596.7 38.6 reduce-scatter.45
  684.1 38.6 reduce-scatter.47
  813.6 38.5 reduce-scatter.51
  906.6 38.6 reduce-scatter.53
  1000.2 38.6 reduce-scatter.55
  1093.6 38.6 reduce-scatter.57
  1188.0 39.8 reduce-scatter.59
  2447.6 349.6 reduce-scatter.87
Sparse Core Ops, SparseCore 1:
  289.1 43.0 all-gather.54
  373.0 44.4 all-gather.56
  463.1 38.1 all-gather.36
  550.0 38.1 all-gather.38
  640.0 38.1 all-gather.40
  727.4 38.0 all-gather.42
  767.0 38.4 all-gather.58
  856.7 38.1 all-gather.44
  953.6 38.1 all-gather.46
  1043.8 38.0 all-gather.48
  1141.6 38.1 all-gather.50
  1190.1 38.7 all-gather.66
  1230.4 38.4 all-gather.68
  1270.6 38.4 all-gather.70
  1311.3 38.4 all-gather.52
  1352.1 38.4 all-gather.60
  1392.3 38.4 all-gather.62
  1432.3 38.4 all-gather.64
  1474.4 71.1 reduce-scatter.81
  1548.0 38.3 reduce-scatter.49
  1590.7 68.7 reduce-scatter.75
  1663.3 70.8 reduce-scatter.83
  1738.3 68.9 reduce-scatter.77
  1810.8 71.3 reduce-scatter.69
  1886.2 71.3 reduce-scatter.71
  1961.2 71.3 reduce-scatter.73
  2036.4 70.8 reduce-scatter.85
  2110.7 68.9 reduce-scatter.79
  2183.2 70.7 reduce-scatter.63
  2257.9 70.7 reduce-scatter.65
  2332.0 70.7 reduce-scatter.67
  2405.3 38.3 reduce-scatter.61
  (1 shorter events, 37.2 us)
where the time goes:
time: 2820 us; the launch traced here: 2810 us
  waiting for transfers between devices  2290 us (81%)
  blocking collectives  249 us (9%)
  matrix products  118 us (4%)
  local copies, waits for them, and re-layouts  65.8 us (2%)
  other arithmetic  61.7 us (2%)
    unnamed x52, waiting for transfers between devices  783 us
    reduce_scatter x6, waiting for transfers between devices, input_back(): lax.psum_scatter(jnp.einsum('sie,de->sid', grad_full, matrix, preferred_e...  226 us
    reduce_scatter x6, waiting for transfers between devices, gather_out(): lax.psum_scatter(jnp.einsum('sie,ed->sid', full_low, matrix, preferred_el...  225 us
    reduce_scatter x3, waiting for transfers between devices, per_device(): lax.psum_scatter(weight_grads[2].astype(jnp.bfloat16), 'dp', scatter_dime...  224 us
    reduce_scatter x3, waiting for transfers between devices, per_device(): lax.psum_scatter(weight_grads[0].astype(jnp.bfloat16), 'dp', scatter_dime...  222 us
    all_gather x6, waiting for transfers between devices, spread_back(): piece = lax.all_gather(grad_low, 'tensor', axis=0, tiled=True)  211 us
    all_gather x6, waiting for transfers between devices, spread_in(): lax.all_gather(rows_low, 'tensor', axis=0, tiled=True)  190 us
    all_gather x1, blocking collectives, per_device(): lax.all_gather(vectors[0], ('dp', 'tensor'), axis=1, tiled=True)  181 us
  transfers between devices with their start and end apart: 49, of which 47 were waited for; matrix products, arithmetic and copies ran while one was open for 4% of the time, Pallas kernels for 0%

commit v1 on v0

v1 whole, which is shorter than its diff:
```python
import jax
import jax.numpy as jnp
from jax import lax
from jax.sharding import Mesh, PartitionSpec as P

HEADS = 16
HDIM = 64

eps = 1e-06
wide = jnp.float32
narrow = jnp.bfloat16


def swap_cores(value):
    return lax.ppermute(value, "core", [(0, 1), (1, 0)])


def along(value, axis, steps):
    count = lax.axis_size(axis)
    return lax.ppermute(value, axis, [(i, (i + steps) % count) for i in range(count)])


def turn(value, flip):
    pairs = []
    for core in range(2):
        for low in range(2):
            pairs.append((core * 2 + low, low * 2 + (core ^ flip)))
    return lax.ppermute(value, ("core", "ylo"), pairs)


def turn_back(value, flip):
    pairs = []
    for core in range(2):
        for low in range(2):
            pairs.append((core * 2 + low, (low ^ flip) * 2 + core))
    return lax.ppermute(value, ("core", "ylo"), pairs)


def gather_tokens(rows):
    count = lax.axis_size("x")
    parts = [rows] + [along(rows, "x", k) for k in range(1, count)]
    mine = jnp.concatenate(parts, axis=0)
    return mine, swap_cores(mine)


def scatter_tokens(make):
    count = lax.axis_size("x")
    arriving = swap_cores(make(1).astype(narrow))
    total = make(0) + arriving.astype(wide)
    rows = total.shape[0] // count
    result = total[:rows]
    sent = [along(total[k * rows : (k + 1) * rows].astype(narrow), "x", -k) for k in range(1, count)]
    for piece in sent:
        result = result + piece.astype(wide)
    return result


def normalise(rows):
    center = rows - jnp.mean(rows, axis=-1, keepdims=True)
    spread = jnp.mean(center * center, axis=-1, keepdims=True)
    inverse = lax.rsqrt(spread + eps)
    return center * inverse, inverse


def norm_back(grad, gain, unit, inverse):
    pulled = grad * gain
    mean_one = jnp.mean(pulled, axis=-1, keepdims=True)
    mean_two = jnp.mean(pulled * unit, axis=-1, keepdims=True)
    return inverse * (pulled - mean_one - unit * mean_two)


def dot(a, b):
    return jnp.dot(a, b, preferred_element_type=wide)


def dot_t(a, b):
    return lax.dot_general(a, b, (((1,), (1,)), ((), ())), preferred_element_type=wide)


def t_dot(a, b):
    return lax.dot_general(a, b, (((0,), (0,)), ((), ())), preferred_element_type=wide)


def heads_of(projected, which, local_width):
    part = projected[:, which * local_width : (which + 1) * local_width]
    return [part[:, h * HDIM : (h + 1) * HDIM] for h in range(local_width // HDIM)]


def attend(projected, local_width, scale):
    mixed, logs = [], []
    for q, k, v in zip(*(heads_of(projected, i, local_width) for i in range(3))):
        scores = dot_t(q, k) * scale
        peak = jnp.max(scores, axis=-1, keepdims=True)
        raised = jnp.exp(scores - peak)
        totals = jnp.sum(raised, axis=-1, keepdims=True)
        probs = (raised / totals).astype(narrow)
        mixed.append(dot(probs, v))
        logs.append(peak + jnp.log(totals))
    return jnp.concatenate(mixed, axis=1).astype(narrow), logs


def attend_back(projected, logs, mixed_grad, local_width, scale):
    query_grads, key_grads, value_grads = [], [], []
    out = [mixed_grad[:, h * HDIM : (h + 1) * HDIM] for h in range(local_width // HDIM)]
    for q, k, v, log_total, o in zip(
        *(heads_of(projected, i, local_width) for i in range(3)), logs, out
    ):
        probs = jnp.exp(dot_t(q, k) * scale - log_total)
        value_grads.append(t_dot(probs.astype(narrow), o))
        prob_grad = dot_t(o, v)
        score_grad = (
            probs * (prob_grad - jnp.sum(probs * prob_grad, axis=-1, keepdims=True))
        ).astype(narrow)
        query_grads.append(dot(score_grad, k) * scale)
        key_grads.append(t_dot(score_grad, q) * scale)
    return jnp.concatenate(query_grads + key_grads + value_grads, axis=1).astype(narrow)


def per_device(inputs, cotangent, qkv_weight, proj_weight, fc1_weight, fc2_weight, vectors):
    width = inputs.shape[3]
    core = lax.axis_index("core")
    low = lax.axis_index("ylo")
    part = core * lax.axis_size("x") + lax.axis_index("x")
    place = lax.axis_index("dp") * 8 + low * lax.axis_size("x") + lax.axis_index("x")
    local_width = qkv_weight.shape[3]
    scale = HDIM ** (-0.5)
    dp = lax.axis_size("dp")

    entering = turn(lax.dynamic_index_in_dim(inputs, core, 0, keepdims=False)[:, 0], 0)
    final_grad = turn(lax.dynamic_index_in_dim(cotangent, core, 0, keepdims=False)[:, 0], 0)

    columns = lax.broadcasted_iota(jnp.int32, (12, width), 1) // 16
    table = jnp.where(columns == place, jnp.tile(vectors[0], (1, width // 16)), 0).astype(narrow)
    for axis in ("x", "ylo", "dp"):
        pieces = [along(table, axis, k) for k in range(1, lax.axis_size(axis))]
        for piece in pieces:
            table = table + piece
    other_table = swap_cores(table)
    tables = [
        jnp.where(core == layer, table, other_table).astype(wide) for layer in range(2)
    ]

    packed = jnp.concatenate(
        [
            jnp.transpose(qkv_weight[0], (1, 0, 2)),
            proj_weight,
            jnp.transpose(fc1_weight[0], (1, 0, 2)),
            fc2_weight[0],
        ],
        axis=0,
    )
    half = packed.shape[1] // 2

    def half_of(which):
        return lax.dynamic_slice_in_dim(packed, which * half, half, 1)

    first, second_piece = turn(half_of(core), 0), turn(half_of(1 - core), 1)
    raw = [jnp.where(low == 0, first, second_piece), jnp.where(low == 0, second_piece, first)]
    weights = []
    for layer in range(2):
        parts = []
        for lo, hi in ((0, 3), (3, 12)):
            parts.append(lax.all_gather(raw[layer][lo:hi], ("dp", "ylo"), axis=0))
        qkv = parts[0].transpose(0, 2, 1, 3) if False else parts[0]
        qkv = jnp.transpose(qkv.reshape(dp, 2, 3, half, local_width), (0, 1, 3, 2, 4))
        qkv = qkv.reshape(width, 3 * local_width)
        rest = parts[1].reshape(dp, 2, 9, half, local_width)
        proj = jnp.transpose(rest[:, :, 0], (1, 2, 0, 3)).reshape(local_width, width)
        fc1 = jnp.transpose(rest[:, :, 1:5], (0, 1, 3, 2, 4)).reshape(width, 4 * local_width)
        fc2 = jnp.transpose(rest[:, :, 5:9], (2, 1, 3, 0, 4)).reshape(4 * local_width, width)
        weights.append((qkv, proj, fc1, fc2))

    def forward(layer, arriving):
        qkv, proj, fc1, fc2 = weights[layer]
        table = tables[layer]
        bias = lax.dynamic_slice_in_dim(table[6:12], part * local_width, local_width, 1)
        qkv_bias = jnp.concatenate([bias[0], jnp.zeros_like(bias[0]), bias[1]])
        fc1_bias = bias[2:6].reshape(4 * local_width)
        unit_one, inverse_one = normalise(arriving)
        normed = gather_tokens((unit_one * table[0] + table[1]).astype(narrow))
        projected = jnp.concatenate(
            [(dot(rows, qkv) + qkv_bias).astype(narrow) for rows in normed], axis=0
        )
        mixed, logs = attend(projected, local_width, scale)
        rows = mixed.shape[0] // 2
        middle = (
            arriving
            + scatter_tokens(lambda h: dot(mixed[h * rows : (h + 1) * rows], proj))
            + table[4]
        )
        unit_two, inverse_two = normalise(middle)
        second = gather_tokens((unit_two * table[2] + table[3]).astype(narrow))
        activated, slope = [], []
        for rows_in in second:
            hidden = dot(rows_in, fc1) + fc1_bias
            share = 0.5 * (1.0 + lax.erf(hidden * (0.5**0.5)))
            activated.append((hidden * share).astype(narrow))
            slope.append(share + hidden * jnp.exp(-0.5 * hidden * hidden) * 0.3989422804014327)
        leaving = middle + scatter_tokens(lambda h: dot(activated[h], fc2)) + table[5]
        kept = (
            unit_one, inverse_one, normed, projected, mixed, logs,
            unit_two, inverse_two, second, activated, slope,
        )
        return leaving.astype(narrow), kept

    def backward(layer, grad, kept):
        qkv, proj, fc1, fc2 = weights[layer]
        table = tables[layer]
        (
            unit_one, inverse_one, normed, projected, mixed, logs,
            unit_two, inverse_two, second, activated, slope,
        ) = kept
        down_grad = grad.astype(narrow)
        down = gather_tokens(down_grad)
        hidden_grad = [(dot_t(down[h], fc2) * slope[h]).astype(narrow) for h in range(2)]
        second_grad = scatter_tokens(lambda h: dot_t(hidden_grad[h], fc1))
        fc2_grad = t_dot(activated[0], down[0]) + t_dot(activated[1], down[1])
        fc1_grad = t_dot(second[0], hidden_grad[0]) + t_dot(second[1], hidden_grad[1])
        middle_grad = grad + norm_back(second_grad, table[2], unit_two, inverse_two)
        branch_grad = middle_grad.astype(narrow)
        branch = gather_tokens(branch_grad)
        mixed_grad = jnp.concatenate([dot_t(rows, proj).astype(narrow) for rows in branch], axis=0)
        rows = mixed.shape[0] // 2
        proj_grad = t_dot(mixed[:rows], branch[0]) + t_dot(mixed[rows:], branch[1])
        projected_grad = attend_back(projected, logs, mixed_grad, local_width, scale)
        normed_grad = scatter_tokens(
            lambda h: dot_t(projected_grad[h * rows : (h + 1) * rows], qkv)
        )
        qkv_grad = t_dot(normed[0], projected_grad[:rows]) + t_dot(normed[1], projected_grad[rows:])
        input_grad = middle_grad + norm_back(normed_grad, table[0], unit_one, inverse_one)

        def total(values):
            return jnp.sum(values.astype(wide), axis=0)

        projected_sums = total(projected_grad).reshape(3, local_width)
        hidden_sums = (total(hidden_grad[0]) + total(hidden_grad[1])).reshape(4, local_width)
        local_rows = jnp.concatenate([projected_sums[0:1], projected_sums[2:3], hidden_sums], axis=0)
        column = lax.broadcasted_iota(jnp.int32, (6, width), 1) // local_width
        placed = jnp.where(column == part, jnp.tile(local_rows, (1, width // local_width)), 0.0)
        shared = jnp.stack(
            [
                total(normed_grad * unit_one),
                total(normed_grad),
                total(second_grad * unit_two),
                total(second_grad),
                total(branch_grad),
                total(down_grad),
            ]
        )
        vector_grad = jnp.concatenate([shared, placed], axis=0)
        pieces = jnp.concatenate(
            [
                jnp.transpose(
                    qkv_grad.astype(narrow).reshape(dp, 2, half, 3, local_width), (0, 1, 3, 2, 4)
                ),
                jnp.transpose(
                    proj_grad.astype(narrow).reshape(1, 2, half, dp, local_width), (3, 1, 0, 2, 4)
                ),
                jnp.transpose(
                    fc1_grad.astype(narrow).reshape(dp, 2, half, 4, local_width), (0, 1, 3, 2, 4)
                ),
                jnp.transpose(
                    fc2_grad.astype(narrow).reshape(4, 2, half, dp, local_width), (3, 1, 0, 2, 4)
                ),
            ],
            axis=2,
        ).reshape(dp * 2, 12, half, local_width)
        owned = lax.psum_scatter(pieces, ("dp", "ylo"), scatter_dimension=0, tiled=False)
        return input_grad, vector_grad, owned

    left_zero, kept_zero = forward(0, entering.astype(wide))
    left_one, kept_one = forward(1, left_zero.astype(wide))
    grad_one, vector_one, owned_one = backward(1, final_grad.astype(wide), kept_one)
    grad_zero, vector_zero, owned_zero = backward(
        0, grad_one.astype(narrow).astype(wide), kept_zero
    )

    mine = jnp.where(low == 0, owned_zero, owned_one)
    other = jnp.where(low == 0, owned_one, owned_zero)
    got_mine, got_other = turn_back(mine, 0), turn_back(other, 1)
    lower = jnp.where(core == 0, got_mine, got_other)
    upper = jnp.where(core == 0, got_other, got_mine)
    blocks = jnp.concatenate([lower, upper], axis=1).astype(wide)

    vector_sum = jnp.where(core == 0, vector_zero, vector_one) + swap_cores(
        jnp.where(core == 0, vector_one, vector_zero)
    )
    for axis in ("x", "ylo", "dp"):
        arrived = [along(vector_sum, axis, k) for k in range(1, lax.axis_size(axis))]
        for piece in arrived:
            vector_sum = vector_sum + piece
    vector_owned = lax.dynamic_slice_in_dim(vector_sum, place * 16, 16, 1)

    def spread(zero, one):
        a = turn(jnp.where(low == 0, zero, one), 0)
        b = turn_back(jnp.where(low == 0, one, zero), 1)
        return jnp.stack([jnp.where(core == 0, a, b), jnp.where(core == 0, b, a)])[None, :, :, None]

    return (
        spread(left_zero, left_one),
        spread(grad_zero, grad_one),
        jnp.transpose(blocks[0:3], (1, 0, 2))[None],
        blocks[3][None],
        jnp.transpose(blocks[4:8], (1, 0, 2))[None],
        blocks[8:12][None],
        vector_owned[None],
    )


def solution(mesh):
    fine = Mesh(mesh.devices.reshape(2, 8, 2, 4), ("core", "dp", "ylo", "x"))
    tensor = ("ylo", "x")
    in_specs = (
        P(None, tensor, "dp", None),
        P(None, tensor, "dp", None),
        P("core", "dp", None, tensor),
        P("core", tensor, "dp"),
        P("core", "dp", None, tensor),
        P("core", None, tensor, "dp"),
        P("core", None, ("dp",) + tensor),
    )
    out_specs = (
        P("core", None, tensor, "dp", None),
        P("core", None, tensor, "dp", None),
        P("core", "dp", None, tensor),
        P("core", tensor, "dp"),
        P("core", "dp", None, tensor),
        P("core", None, tensor, "dp"),
        P("core", None, ("dp",) + tensor),
    )
    return jax.shard_map(
        per_device, mesh=fine, in_specs=in_specs, out_specs=out_specs, check_vma=False
    )
```

time: 2820 us -> 499 us (0.18)
  waiting for transfers between devices: 2290 us -> 159 us
  blocking collectives: 249 us -> 47.9 us
  starting transfers between devices: 8.51 us -> 117 us
  matrix products: 118 us -> 63.5 us
    reduce_scatter x18 -> x0, waiting for transfers between devices: 897 us -> none  [the longest x6 226 us: input_back(): lax.psum_scatter(jnp.einsum('sie,de->sid', grad_full, matrix, preferred_e...]
    unnamed x52 -> x6, waiting for transfers between devices: 783 us -> 19.3 us
    all_gather x20 -> x2, waiting for transfers between devices: 599 us -> 0.01 us  [per_device(): parts.append(lax.all_gather(raw[layer][lo:hi], ('dp', 'ylo'), axis=0))]
    all_gather x3 -> x2, blocking collectives: 249 us -> 47.9 us  [per_device(): parts.append(lax.all_gather(raw[layer][lo:hi], ('dp', 'ylo'), axis=0))]
    ppermute x4 -> x98, waiting for transfers between devices: 5.89 us -> 140 us  [the longest x70 130 us: along(): lax.ppermute(value, axis, [(i, (i + steps) % count) for i in range(count)])]
    ppermute x4 -> x98, starting transfers between devices: 5.16 us -> 117 us  [the longest x70 95.8 us: along(): lax.ppermute(value, axis, [(i, (i + steps) % count) for i in range(count)])]
    dot_general x57 -> x72, matrix products: 118 us -> 63.5 us  [the longest x24 22.9 us: dot_t(): lax.dot_general(a, b, (((1,), (1,)), ((), ())), preferred_element_type=wide)]
  transfers between devices with their start and end apart: 49 -> 102, of which waited for: 47 -> 58; matrix products, arithmetic and copies ran while one was open for 4% -> 26% of each run, Pallas kernels for 0% -> 0%
where the time goes in v1:
time: 499 us; the launch traced here: 489 us
  waiting for transfers between devices  159 us (32%)
  starting transfers between devices  117 us (23%)
  matrix products  63.5 us (13%)
  local copies, waits for them, and re-layouts  49.6 us (10%)
  blocking collectives  47.9 us (10%)
  other arithmetic  34.9 us (7%)
  between operations  16.7 us (3%)
    ppermute x70, waiting for transfers between devices, along(): lax.ppermute(value, axis, [(i, (i + steps) % count) for i in range(count)])  130 us
    ppermute x70, starting transfers between devices, along(): lax.ppermute(value, axis, [(i, (i + steps) % count) for i in range(count)])  95.8 us
    all_gather x2, blocking collectives, per_device(): parts.append(lax.all_gather(raw[layer][lo:hi], ('dp', 'ylo'), axis=0))  47.9 us
    dot_general x24, matrix products, dot_t(): lax.dot_general(a, b, (((1,), (1,)), ((), ())), preferred_element_type=wide)  22.9 us
    dot_general x24, matrix products, t_dot(): lax.dot_general(a, b, (((0,), (0,)), ((), ())), preferred_element_type=wide)  22.6 us
    unnamed x6, waiting for transfers between devices  19.3 us
    dot_general x24, matrix products, dot(): return jnp.dot(a, b, preferred_element_type=wide)  18 us
    unnamed x278, local copies, waits for them, and re-layouts  13.4 us
  transfers between devices with their start and end apart: 102, of which 58 were waited for; matrix products, arithmetic and copies ran while one was open for 26% of the time, Pallas kernels for 0%

profile of v1, /device:TPU:0, one launch (start us, length us, event | category | flops | bytes accessed | tf_op | source)
XLA Modules:
  0.0 489.0 jit_solution(1924060288059031564)
XLA Ops:
  19.7 4.2 collective-permute-done.4
  23.9 6.7 %collective-permute-start.11 = (bf16[12,1024]{1,0:T(8,128)(2,1)S(1)}, bf16[12,1024]{1,0:T(8,128)(2,1)S(1)}, u32[]{:S(2)}, u32[]{:S(2)}) collective-permute-start(bf16[12,1024]{1,0:T(8,128)(2,1)S(1)} %add.497), channel_id=1, source_target_pairs={{0,56},{8,0},{16,8},{24,16},{32,24},{40,32},{48,40},{56,48},{1,57}... | collective-permute-start | bytes 73736 | tf_op jit(solution)/shard_map/ppermute | solution.py:20
  34.5 4.5 collective-permute-start.7
  59.8 3.7 collective-permute-start.18
  64.1 25.0 %all-gather = bf16[48,64,128]{2,1,0:T(8,128)(2,1)S(1)} all-gather(bf16[3,64,128]{2,1,0:T(8,128)(2,1)S(1)} %slice.466), channel_id=2, replica_groups=mesh['core'=2,'dp'=8,'ylo'=2,'x'=4] {'dp','ylo'}, dimensions={0}, use_global_device_ids=true | all-gather | bytes 835584 | tf_op jit(solution)/shard_map/all_gather | solution.py:163
  104.9 6.0 %collective-permute-done.22 = bf16[72,1024]{1,0:T(8,128)(2,1)S(1)} collective-permute-done((bf16[72,1024]{1,0:T(8,128)(2,1)S(1)}, bf16[72,1024]{1,0:T(8,128)(2,1)S(1)}, u32[]{:S(2)}, u32[]{:S(2)}) %collective-permute-start.22) | collective-permute-done | bytes 147488 | tf_op jit(solution)/shard_map/ppermute | solution.py:20
  117.0 4.7 collective-permute-done.25
  139.2 5.4 %collective-permute-done.30 = bf16[72,1024]{1,0:T(8,128)(2,1)S(1)} collective-permute-done((bf16[72,1024]{1,0:T(8,128)(2,1)S(1)}, bf16[72,1024]{1,0:T(8,128)(2,1)S(1)}, u32[]{:S(2)}, u32[]{:S(2)}) %collective-permute-start.30) | collective-permute-done | bytes 147488 | tf_op jit(solution)/shard_map/ppermute | solution.py:20
  149.7 5.2 %collective-permute-done.33 = bf16[72,1024]{1,0:T(8,128)(2,1)S(1)} collective-permute-done((bf16[72,1024]{1,0:T(8,128)(2,1)S(1)}, bf16[72,1024]{1,0:T(8,128)(2,1)S(1)}, u32[]{:S(2)}, u32[]{:S(2)}) %collective-permute-start.33) | collective-permute-done | bytes 147488 | tf_op jit(solution)/shard_map/ppermute | solution.py:20
  160.0 22.9 %all-gather.2 = bf16[48,64,128]{2,1,0:T(8,128)(2,1)S(1)} all-gather(bf16[3,64,128]{2,1,0:T(8,128)(2,1)S(1)} %slice.498), channel_id=4, replica_groups=mesh['core'=2,'dp'=8,'ylo'=2,'x'=4] {'dp','ylo'}, dimensions={0}, use_global_device_ids=true | all-gather | bytes 835584 | tf_op jit(solution)/shard_map/all_gather | solution.py:163
  200.9 4.5 collective-permute-done.38
  211.8 4.3 collective-permute-done.41
  228.1 3.5 collective-permute-start.56
  231.6 4.0 collective-permute-done.57
  235.7 3.3 collective-permute-done.56
  245.0 5.6 %collective-permute-done.60 = bf16[72,1024]{1,0:T(8,128)(2,1)S(1)} collective-permute-done((bf16[72,1024]{1,0:T(8,128)(2,1)S(1)}, bf16[72,1024]{1,0:T(8,128)(2,1)S(1)}, u32[]{:S(2)}, u32[]{:S(2)}) %collective-permute-start.60) | collective-permute-done | bytes 147488 | tf_op jit(solution)/shard_map/ppermute | solution.py:20
  286.9 5.0 %collective-permute-done.68 = bf16[72,1024]{1,0:T(8,128)(2,1)S(1)} collective-permute-done((bf16[72,1024]{1,0:T(8,128)(2,1)S(1)}, bf16[72,1024]{1,0:T(8,128)(2,1)S(1)}, u32[]{:S(2)}, u32[]{:S(2)}) %collective-permute-start.68) | collective-permute-done | bytes 147488 | tf_op jit(solution)/shard_map/ppermute | solution.py:20
  302.2 3.2 reshape.257
  310.1 3.3 pad_maximum_fusion.1
  325.9 5.4 %collective-permute-done.73 = bf16[72,1024]{1,0:T(8,128)(2,1)S(1)} collective-permute-done((bf16[72,1024]{1,0:T(8,128)(2,1)S(1)}, bf16[72,1024]{1,0:T(8,128)(2,1)S(1)}, u32[]{:S(2)}, u32[]{:S(2)}) %collective-permute-start.73) | collective-permute-done | bytes 147488 | tf_op jit(solution)/shard_map/ppermute | solution.py:20
  338.4 4.7 collective-permute-done.76
  372.2 4.2 pad_maximum_fusion
  385.6 7.0 %collective-permute-done.46 = bf16[72,1024]{1,0:T(8,128)(2,1)S(1)} collective-permute-done((bf16[72,1024]{1,0:T(8,128)(2,1)S(1)}, bf16[72,1024]{1,0:T(8,128)(2,1)S(1)}, u32[]{:S(2)}, u32[]{:S(2)}) %collective-permute-start.46) | collective-permute-done | bytes 147488 | tf_op jit(solution)/shard_map/ppermute | solution.py:20
  401.8 3.6 collective-permute-start.80
  405.7 3.1 collective-permute-done.81
  408.8 3.6 collective-permute-done.80
  428.7 3.0 collective-permute-start.97
  437.1 3.9 collective-permute-start.94
  442.0 3.0 collective-permute-start.83
  445.0 4.1 collective-permute-done.93
  449.8 19.2 %reduce-scatter.7.cloned.1.call-done = bf16[1,12,64,128]{3,2,1,0:T(8,128)(2,1)} async-done(((bf16[16,12,64,128]{3,2,1,0:T(8,128)(2,1)}), bf16[1,12,64,128]{3,2,1,0:T(8,128)(2,1)}) %reduce-scatter.7.cloned.1.call-update) | async-done | bytes 196624
  474.9 4.0 collective-permute-done.85
  (671 shorter events, 278.4 us)
Async XLA Ops:
  7.2 87.9 %all-gather.7.cloned.1.call-start = ((), (), s32[]{:S(2)}) async-start(), calls=%async_computation.2 | async-start | bytes 2506752 | tf_op jit(solution)/shard_map/all_gather | solution.py:163
  15.4 23.6 %collective-permute-start.17 = (bf16[12,64,128]{2,1,0:T(8,128)(2,1)S(1)}, bf16[12,64,128]{2,1,0:T(8,128)(2,1)S(1)}, u32[]{:S(2)}, u32[]{:S(2)}) collective-permute-start(bf16[12,64,128]{2,1,0:T(8,128)(2,1)S(1)} %get-tuple-element.105), channel_id=1, source_target_pairs={{0,4},{4,68},{64,0},{68,64},{1,5},{5,69},{65,1},{69,65},{2,6},{6,7... | collective-permute-start | bytes 589832 | tf_op jit(solution)/shard_map/ppermute | solution.py:28
  17.1 21.9 %collective-permute-start.16 = (bf16[12,64,128]{2,1,0:T(8,128)(2,1)S(1)}, bf16[12,64,128]{2,1,0:T(8,128)(2,1)S(1)}, u32[]{:S(2)}, u32[]{:S(2)}) collective-permute-start(bf16[12,64,128]{2,1,0:T(8,128)(2,1)S(1)} %get-tuple-element.106), channel_id=1, source_target_pairs={{0,0},{4,64},{64,4},{68,68},{1,1},{5,65},{65,5},{69,69},{2,2},{6,6... | collective-permute-start | bytes 589832 | tf_op jit(solution)/shard_map/ppermute | solution.py:28
  31.0 11.0 %collective-permute-start.9 = (bf16[12,1024]{1,0:T(8,128)(2,1)S(1)}, bf16[12,1024]{1,0:T(8,128)(2,1)S(1)}, u32[]{:S(2)}, u32[]{:S(2)}) collective-permute-start(bf16[12,1024]{1,0:T(8,128)(2,1)S(1)} %add.497), channel_id=1, source_target_pairs={{0,40},{8,48},{16,56},{24,0},{32,8},{40,16},{48,24},{56,32},{1,41}... | collective-permute-start | bytes 73736 | tf_op jit(solution)/shard_map/ppermute | solution.py:20
  42.0 142.6 %all-gather.9.cloned.1.call-start = ((), (), s32[]{:S(2)}) async-start(), calls=%async_computation.3 | async-start | bytes 2506752 | tf_op jit(solution)/shard_map/all_gather | solution.py:163
  59.8 30.6 %collective-permute-start.18 = (bf16[288,1024]{1,0:T(8,128)(2,1)S(1)}, bf16[288,1024]{1,0:T(8,128)(2,1)S(1)}, u32[]{:S(2)}, u32[]{:S(2)}) collective-permute-start(bf16[288,1024]{1,0:T(8,128)(2,1)S(1)} %pad_maximum_fusion.2), channel_id=1, source_target_pairs={{0,64},{64,0},{1,65},{65,1},{2,66},{66,2},{3,67},{67,3},{4,68},{68... | collective-permute-start | bytes 1769480 | tf_op jit(solution)/shard_map/ppermute | solution.py:15
  100.6 10.3 %collective-permute-start.22 = (bf16[72,1024]{1,0:T(8,128)(2,1)S(1)}, bf16[72,1024]{1,0:T(8,128)(2,1)S(1)}, u32[]{:S(2)}, u32[]{:S(2)}) collective-permute-start(bf16[72,1024]{1,0:T(8,128)(2,1)S(1)} %get-tuple-element.97), channel_id=1, source_target_pairs={{0,1},{1,2},{2,3},{3,0},{4,5},{5,6},{6,7},{7,4},{8,9},{9,10},{10,1... | collective-permute-start | bytes 442376 | tf_op jit(solution)/shard_map/ppermute | solution.py:20
  116.9 332.9 %reduce-scatter.9.cloned.1.call-start = ((), (), s32[]{:S(2)}) async-start(), calls=%async_computation.5 | async-start | bytes 3342336
  134.3 10.3 %collective-permute-start.30 = (bf16[72,1024]{1,0:T(8,128)(2,1)S(1)}, bf16[72,1024]{1,0:T(8,128)(2,1)S(1)}, u32[]{:S(2)}, u32[]{:S(2)}) collective-permute-start(bf16[72,1024]{1,0:T(8,128)(2,1)S(1)} %get-tuple-element.94), channel_id=1, source_target_pairs={{0,1},{1,2},{2,3},{3,0},{4,5},{5,6},{6,7},{7,4},{8,9},{9,10},{10,1... | collective-permute-start | bytes 442376 | tf_op jit(solution)/shard_map/ppermute | solution.py:20
  134.4 10.2 %collective-permute-start.29 = (bf16[72,1024]{1,0:T(8,128)(2,1)S(1)}, bf16[72,1024]{1,0:T(8,128)(2,1)S(1)}, u32[]{:S(2)}, u32[]{:S(2)}) collective-permute-start(bf16[72,1024]{1,0:T(8,128)(2,1)S(1)} %get-tuple-element.95), channel_id=1, source_target_pairs={{0,2},{1,3},{2,0},{3,1},{4,6},{5,7},{6,4},{7,5},{8,10},{9,11},{10,... | collective-permute-start | bytes 442376 | tf_op jit(solution)/shard_map/ppermute | solution.py:20
  159.2 28.7 %collective-permute-start.34 = (bf16[288,1024]{1,0:T(8,128)(2,1)}, bf16[288,1024]{1,0:T(8,128)(2,1)}, u32[]{:S(2)}, u32[]{:S(2)}) collective-permute-start(bf16[288,1024]{1,0:T(8,128)(2,1)} %pad_maximum_fusion.4), channel_id=1, source_target_pairs={{0,64},{64,0},{1,65},{65,1},{2,66},{66,2},{3,67},{67,3},{4,68},{68... | collective-permute-start | bytes 1769480 | tf_op jit(solution)/shard_map/ppermute | solution.py:15
  194.5 10.9 %collective-permute-start.38 = (bf16[72,1024]{1,0:T(8,128)(2,1)S(1)}, bf16[72,1024]{1,0:T(8,128)(2,1)S(1)}, u32[]{:S(2)}, u32[]{:S(2)}) collective-permute-start(bf16[72,1024]{1,0:T(8,128)(2,1)S(1)} %get-tuple-element.91), channel_id=1, source_target_pairs={{0,1},{1,2},{2,3},{3,0},{4,5},{5,6},{6,7},{7,4},{8,9},{9,10},{10,1... | collective-permute-start | bytes 442376 | tf_op jit(solution)/shard_map/ppermute | solution.py:20
  194.6 10.8 %collective-permute-start.37 = (bf16[72,1024]{1,0:T(8,128)(2,1)S(1)}, bf16[72,1024]{1,0:T(8,128)(2,1)S(1)}, u32[]{:S(2)}, u32[]{:S(2)}) collective-permute-start(bf16[72,1024]{1,0:T(8,128)(2,1)S(1)} %get-tuple-element.92), channel_id=1, source_target_pairs={{0,2},{1,3},{2,0},{3,1},{4,6},{5,7},{6,4},{7,5},{8,10},{9,11},{10,... | collective-permute-start | bytes 442376 | tf_op jit(solution)/shard_map/ppermute | solution.py:20
  197.8 13.9 %collective-permute-start.50 = (bf16[72,1024]{1,0:T(8,128)(2,1)S(1)}, bf16[72,1024]{1,0:T(8,128)(2,1)S(1)}, u32[]{:S(2)}, u32[]{:S(2)}) collective-permute-start(bf16[72,1024]{1,0:T(8,128)(2,1)S(1)} %collective-permute-done.49), channel_id=1, source_target_pairs={{0,1},{1,2},{2,3},{3,0},{4,5},{5,6},{6,7},{7,4},{8,9},{9,10},{10,1... | collective-permute-start | bytes 442376 | tf_op jit(solution)/shard_map/ppermute | solution.py:20
  199.0 12.7 %collective-permute-start.51 = (bf16[72,1024]{1,0:T(8,128)(2,1)S(1)}, bf16[72,1024]{1,0:T(8,128)(2,1)S(1)}, u32[]{:S(2)}, u32[]{:S(2)}) collective-permute-start(bf16[72,1024]{1,0:T(8,128)(2,1)S(1)} %collective-permute-done.49), channel_id=1, source_target_pairs={{0,2},{1,3},{2,0},{3,1},{4,6},{5,7},{6,4},{7,5},{8,10},{9,11},{10,... | collective-permute-start | bytes 442376 | tf_op jit(solution)/shard_map/ppermute | solution.py:20
  205.4 14.6 %collective-permute-start.52 = (bf16[72,1024]{1,0:T(8,128)(2,1)S(1)}, bf16[72,1024]{1,0:T(8,128)(2,1)S(1)}, u32[]{:S(2)}, u32[]{:S(2)}) collective-permute-start(bf16[72,1024]{1,0:T(8,128)(2,1)S(1)} %collective-permute-done.49), channel_id=1, source_target_pairs={{0,3},{1,0},{2,1},{3,2},{4,7},{5,4},{6,5},{7,6},{8,11},{9,8},{10,9... | collective-permute-start | bytes 442376 | tf_op jit(solution)/shard_map/ppermute | solution.py:20
  228.1 10.8 %collective-permute-start.56 = (bf16[72,1024]{1,0:T(8,128)(2,1)S(1)}, bf16[72,1024]{1,0:T(8,128)(2,1)S(1)}, u32[]{:S(2)}, u32[]{:S(2)}) collective-permute-start(bf16[72,1024]{1,0:T(8,128)(2,1)S(1)} %get-tuple-element.86), channel_id=1, source_target_pairs={{0,2},{1,3},{2,0},{3,1},{4,6},{5,7},{6,4},{7,5},{8,10},{9,11},{10,... | collective-permute-start | bytes 442376 | tf_op jit(solution)/shard_map/ppermute | solution.py:20
  244.2 9.8 %collective-permute-start.58 = (bf16[72,1024]{1,0:T(8,128)(2,1)S(1)}, bf16[72,1024]{1,0:T(8,128)(2,1)S(1)}, u32[]{:S(2)}, u32[]{:S(2)}) collective-permute-start(bf16[72,1024]{1,0:T(8,128)(2,1)S(1)} %get-tuple-element.51), channel_id=1, source_target_pairs={{0,1},{1,2},{2,3},{3,0},{4,5},{5,6},{6,7},{7,4},{8,9},{9,10},{10,1... | collective-permute-start | bytes 442376 | tf_op jit(solution)/shard_map/ppermute | solution.py:20
  255.5 123.5 %collective-permute-start.43 = (bf16[288,1024]{1,0:T(8,128)(2,1)}, bf16[288,1024]{1,0:T(8,128)(2,1)}, u32[]{:S(2)}, u32[]{:S(2)}) collective-permute-start(bf16[288,1024]{1,0:T(8,128)(2,1)} %convolution_convert_fusion.6), channel_id=1, source_target_pairs={{0,64},{64,0},{1,65},{65,1},{2,66},{66,2},{3,67},{67,3},{4,68},{68... | collective-permute-start | bytes 1769480 | tf_op jit(solution)/shard_map/ppermute | solution.py:15
  267.4 10.9 %collective-permute-start.65 = (bf16[72,1024]{1,0:T(8,128)(2,1)}, bf16[72,1024]{1,0:T(8,128)(2,1)}, u32[]{:S(2)}, u32[]{:S(2)}) collective-permute-start(bf16[72,1024]{1,0:T(8,128)(2,1)} %get-tuple-element.82), channel_id=1, source_target_pairs={{0,1},{1,2},{2,3},{3,0},{4,5},{5,6},{6,7},{7,4},{8,9},{9,10},{10,1... | collective-permute-start | bytes 442376 | tf_op jit(solution)/shard_map/ppermute | solution.py:20
  267.4 10.9 %collective-permute-start.64 = (bf16[72,1024]{1,0:T(8,128)(2,1)}, bf16[72,1024]{1,0:T(8,128)(2,1)}, u32[]{:S(2)}, u32[]{:S(2)}) collective-permute-start(bf16[72,1024]{1,0:T(8,128)(2,1)} %get-tuple-element.83), channel_id=1, source_target_pairs={{0,2},{1,3},{2,0},{3,1},{4,6},{5,7},{6,4},{7,5},{8,10},{9,11},{10,... | collective-permute-start | bytes 442376 | tf_op jit(solution)/shard_map/ppermute | solution.py:20
  315.9 153.2 %reduce-scatter.7.cloned.1.call-start = ((), (), s32[]{:S(2)}) async-start(), calls=%async_computation.4 | async-start | bytes 3342336
  320.6 10.6 %collective-permute-start.73 = (bf16[72,1024]{1,0:T(8,128)(2,1)S(1)}, bf16[72,1024]{1,0:T(8,128)(2,1)S(1)}, u32[]{:S(2)}, u32[]{:S(2)}) collective-permute-start(bf16[72,1024]{1,0:T(8,128)(2,1)S(1)} %get-tuple-element.79), channel_id=1, source_target_pairs={{0,1},{1,2},{2,3},{3,0},{4,5},{5,6},{6,7},{7,4},{8,9},{9,10},{10,1... | collective-permute-start | bytes 442376 | tf_op jit(solution)/shard_map/ppermute | solution.py:20
  320.7 10.6 %collective-permute-start.72 = (bf16[72,1024]{1,0:T(8,128)(2,1)S(1)}, bf16[72,1024]{1,0:T(8,128)(2,1)S(1)}, u32[]{:S(2)}, u32[]{:S(2)}) collective-permute-start(bf16[72,1024]{1,0:T(8,128)(2,1)S(1)} %get-tuple-element.80), channel_id=1, source_target_pairs={{0,2},{1,3},{2,0},{3,1},{4,6},{5,7},{6,4},{7,5},{8,10},{9,11},{10,... | collective-permute-start | bytes 442376 | tf_op jit(solution)/shard_map/ppermute | solution.py:20
  382.0 10.6 %collective-permute-start.46 = (bf16[72,1024]{1,0:T(8,128)(2,1)S(1)}, bf16[72,1024]{1,0:T(8,128)(2,1)S(1)}, u32[]{:S(2)}, u32[]{:S(2)}) collective-permute-start(bf16[72,1024]{1,0:T(8,128)(2,1)S(1)} %get-tuple-element.88), channel_id=1, source_target_pairs={{0,1},{1,2},{2,3},{3,0},{4,5},{5,6},{6,7},{7,4},{8,9},{9,10},{10,1... | collective-permute-start | bytes 442376 | tf_op jit(solution)/shard_map/ppermute | solution.py:20
  382.0 10.6 %collective-permute-start.45 = (bf16[72,1024]{1,0:T(8,128)(2,1)S(1)}, bf16[72,1024]{1,0:T(8,128)(2,1)S(1)}, u32[]{:S(2)}, u32[]{:S(2)}) collective-permute-start(bf16[72,1024]{1,0:T(8,128)(2,1)S(1)} %get-tuple-element.89), channel_id=1, source_target_pairs={{0,2},{1,3},{2,0},{3,1},{4,6},{5,7},{6,4},{7,5},{8,10},{9,11},{10,... | collective-permute-start | bytes 442376 | tf_op jit(solution)/shard_map/ppermute | solution.py:20
  394.2 19.6 %collective-permute-start.47 = (bf16[72,1024]{1,0:T(8,128)(2,1)}, bf16[72,1024]{1,0:T(8,128)(2,1)}, u32[]{:S(2)}, u32[]{:S(2)}) collective-permute-start(bf16[72,1024]{1,0:T(8,128)(2,1)} %get-tuple-element.57), channel_id=1, source_target_pairs={{0,0},{4,64},{64,4},{68,68},{1,1},{5,65},{65,5},{69,69},{2,2},{6,6... | collective-permute-start | bytes 442376 | tf_op jit(solution)/shard_map/ppermute | solution.py:28
  397.8 16.1 %collective-permute-start.48 = (bf16[72,1024]{1,0:T(8,128)(2,1)}, bf16[72,1024]{1,0:T(8,128)(2,1)S(1)}, u32[]{:S(2)}, u32[]{:S(2)}) collective-permute-start(bf16[72,1024]{1,0:T(8,128)(2,1)} %broadcast_select_fusion.6), channel_id=1, source_target_pairs={{0,64},{4,0},{64,68},{68,4},{1,65},{5,1},{65,69},{69,5},{2,66},{6,... | collective-permute-start | bytes 442376 | tf_op jit(solution)/shard_map/ppermute | solution.py:36
  401.8 10.7 %collective-permute-start.80 = (bf16[72,1024]{1,0:T(8,128)(2,1)S(1)}, bf16[72,1024]{1,0:T(8,128)(2,1)S(1)}, u32[]{:S(2)}, u32[]{:S(2)}) collective-permute-start(bf16[72,1024]{1,0:T(8,128)(2,1)S(1)} %get-tuple-element.77), channel_id=1, source_target_pairs={{0,2},{1,3},{2,0},{3,1},{4,6},{5,7},{6,4},{7,5},{8,10},{9,11},{10,... | collective-permute-start | bytes 442376 | tf_op jit(solution)/shard_map/ppermute | solution.py:20
  428.7 12.2 %collective-permute-start.97 = (f32[12,1024]{1,0:T(8,128)S(1)}, f32[12,1024]{1,0:T(8,128)S(1)}, u32[]{:S(2)}, u32[]{:S(2)}) collective-permute-start(f32[12,1024]{1,0:T(8,128)S(1)} %add.618), channel_id=1, source_target_pairs={{0,56},{8,0},{16,8},{24,16},{32,24},{40,32},{48,40},{56,48},{1,57}... | collective-permute-start | bytes 147464 | tf_op jit(solution)/shard_map/ppermute | solution.py:20
  441.3 32.1 %collective-permute-start.82 = (f32[72,1024]{1,0:T(8,128)S(1)}, f32[72,1024]{1,0:T(8,128)S(1)}, u32[]{:S(2)}, u32[]{:S(2)}) collective-permute-start(f32[72,1024]{1,0:T(8,128)S(1)} %get-tuple-element.69), channel_id=1, source_target_pairs={{0,0},{4,64},{64,4},{68,68},{1,1},{5,65},{65,5},{69,69},{2,2},{6,6... | collective-permute-start | bytes 884744 | tf_op jit(solution)/shard_map/ppermute | solution.py:28
  442.0 31.4 %collective-permute-start.83 = (f32[72,1024]{1,0:T(8,128)S(1)}, f32[72,1024]{1,0:T(8,128)S(1)}, u32[]{:S(2)}, u32[]{:S(2)}) collective-permute-start(f32[72,1024]{1,0:T(8,128)S(1)} %get-tuple-element.70), channel_id=1, source_target_pairs={{0,64},{4,0},{64,68},{68,4},{1,65},{5,1},{65,69},{69,5},{2,66},{6,... | collective-permute-start | bytes 884744 | tf_op jit(solution)/shard_map/ppermute | solution.py:36
  (200 other events, 1927.3 us)
Sparse Core Ops, SparseCore 0:
  42.1 48.5 all-gather.6
  117.1 44.0 all-gather.8
  316.0 72.4 reduce-scatter.8
  391.7 77.3 reduce-scatter.6
